TPU v7x, 32 devices: a whole 2x2x4 slice. The times are simulated.
32 devices in a mesh: lat: 8 (over z, y), tok: 4 (over x, core).
Axes of the slice: x: 2, y: 2, z: 4, core: 2. Of those that a mesh axis runs over, the one named last changes fastest.
Arguments:
- resid: bfloat16 [8192, 512], P('lat', 'tok'), may hold values from -6 to 6
- active_ids: int32 [512, 64], P('tok'), may hold values from 0 to 16383, all different within a row
- w_enc: bfloat16 [16384, 8192], P('lat', 'tok'), may hold values from -0.5 to 0.5
- w_dec: bfloat16 [16384, 8192], P('lat', 'tok'), may hold values from -0.0625 to 0.0625
- b_enc: float32 [16384], P('lat'), may hold values from -8 to 8
- b_dec: bfloat16 [8192], P('lat'), may hold values from -3 to 3
Outputs:
- grad_w_enc: bfloat16 [16384, 8192], P('lat', 'tok')
- grad_w_dec: bfloat16 [16384, 8192], P('lat', 'tok')
- grad_b_enc: float32 [16384], P('lat')
- grad_b_dec: float32 [8192], P('tok')
Inputs may be any that keep to these rules, and one draw needn't show every extreme that they name: `active_ids`: the 64 latents of a token are distinct, and every latent is active for some token.
All inputs are finite; a program needn't handle non-finite values.
Results may differ from a plain program's by a relative error of at most 0.0068.
Values may be sent and summed in bfloat16 or wider, within the bound.
A program may use at most 256 MiB of HBM per device.

v0:
```python
import jax
import jax.numpy as jnp
from jax import lax
from jax.sharding import PartitionSpec as P

f32 = jnp.float32
bf16 = jnp.bfloat16


def active_rows(ids, base, rows):
    word = 32 if rows % 32 == 0 else rows
    local = ids - base
    which = local // word
    place = local - which * word
    bit = lax.shift_left(jnp.int32(1), place)
    words = lax.iota(jnp.int32, rows // word)
    held = jnp.where(which[None, :, :] == words[:, None, None], bit[None, :, :], 0)
    held = jnp.sum(held, axis=1)
    shifts = lax.iota(jnp.int32, word)
    flags = (
        lax.shift_right_logical(
            held[:, None, :],
            jnp.broadcast_to(shifts[None, :, None], (rows // word, word, held.shape[1])),
        )
        & 1
    )
    return flags.reshape(rows, held.shape[1]).astype(f32)


def on_device(resid, active_ids, w_enc, w_dec, b_enc, b_dec):
    block_rows = w_enc.shape[0]
    width = w_enc.shape[1]
    lat_pos = lax.axis_index("lat")
    tok_pos = lax.axis_index("tok")
    tok_count = lax.axis_size("tok")
    lat_count = lax.axis_size("lat")
    rows = block_rows // tok_count
    feats = width // lat_count
    ids_all = lax.all_gather(active_ids, "tok", axis=0, tiled=True).T
    bias_full = lax.all_gather(b_dec, "lat", axis=0, tiled=True)
    resid_full = lax.all_gather(resid, "lat", axis=0, tiled=True)
    resid_mine = lax.all_to_all(resid_full, "tok", split_axis=0, concat_axis=1, tiled=True)
    bias_mine = lax.dynamic_slice_in_dim(bias_full, tok_pos * width, width, 0)
    centred = (resid_mine.astype(f32) - bias_mine.astype(f32)[:, None]).astype(bf16)
    active = active_rows(ids_all, lat_pos * block_rows + tok_pos * rows, rows)
    b_rows = lax.dynamic_slice_in_dim(b_enc, tok_pos * rows, rows, 0)
    pre_part = jnp.dot(w_enc, centred, preferred_element_type=f32).astype(bf16)
    pre = lax.psum_scatter(pre_part, "tok", scatter_dimension=0, tiled=True)
    codes_rows = ((pre.astype(f32) + b_rows[:, None]) * active).astype(bf16)
    codes = lax.all_gather(codes_rows, "tok", axis=0, tiled=True)
    recon_part = lax.dot_general(
        w_dec, codes, (((0,), (0,)), ((), ())), preferred_element_type=f32
    ).astype(bf16)
    recon = lax.psum_scatter(recon_part, "lat", scatter_dimension=0, tiled=True)
    r_rows = lax.dynamic_slice_in_dim(resid_mine, lat_pos * feats, feats, 0)
    bd_rows = lax.dynamic_slice_in_dim(bias_mine, lat_pos * feats, feats, 0)
    error_rows = (recon.astype(f32) + bd_rows.astype(f32)[:, None] - r_rows.astype(f32)).astype(
        bf16
    )
    errors = lax.all_gather(error_rows, "lat", axis=0, tiled=True)
    gc_part = jnp.dot(w_dec, errors, preferred_element_type=f32).astype(bf16)
    gc = lax.psum_scatter(gc_part, "tok", scatter_dimension=0, tiled=True)
    gp_rows = (gc.astype(f32) * active).astype(bf16)
    grad_pre = lax.all_gather(gp_rows, "tok", axis=0, tiled=True)
    grad_w_dec = lax.dot_general(
        codes, errors, (((1,), (1,)), ((), ())), preferred_element_type=f32
    ).astype(bf16)
    grad_b_enc = jnp.sum(grad_pre.astype(f32), axis=1)
    high = grad_b_enc.astype(bf16)
    rest = grad_b_enc - high.astype(f32)
    mid = rest.astype(bf16)
    low = (rest - mid.astype(f32)).astype(bf16)
    parts = jnp.stack([high, mid, low])
    back = jnp.sum(jnp.dot(parts, w_enc, preferred_element_type=f32), axis=0)
    back = lax.psum(back, "lat")
    error_total = jnp.sum(errors.astype(f32), axis=1)
    grad_w_enc = lax.dot_general(
        grad_pre, centred, (((1,), (1,)), ((), ())), preferred_element_type=f32
    ).astype(bf16)
    return (grad_w_enc, grad_w_dec, grad_b_enc, error_total - back)


def solution(mesh):
    return jax.shard_map(
        on_device,
        mesh=mesh,
        in_specs=(
            P("lat", "tok"),
            P("tok", None),
            P("lat", "tok"),
            P("lat", "tok"),
            P("lat"),
            P("lat"),
        ),
        out_specs=(P("lat", "tok"), P("lat", "tok"), P("lat"), P("tok")),
        check_vma=False,
    )
```

profile of v0, /device:TPU:0, one launch (start us, length us, event | category | flops | bytes accessed | tf_op | source)
XLA Modules:
  0.0 399.6 jit_solution(10416619332048094439)
XLA Ops:
  7.2 0.7 all-gather.5.cloned.1.call-update
  7.9 54.2 %all-gather.5.cloned.1.call-done = bf16[8192,128]{1,0:T(8,128)(2,1)} async-done(((bf16[1024,128]{1,0:T(8,128)(2,1)}), bf16[8192,128]{1,0:T(8,128)(2,1)}) %all-gather.5.cloned.1.call-update) | async-done | bytes 2097168 | tf_op jit(solution)/shard_map/all_gather | solution.py:41
  62.1 3.9 copy.15
  66.1 3.7 all-to-all-start
  69.9 26.0 %all_gather.19 = bf16[8192]{0:T(1024)(128)(2,1)S(1)} all-gather(bf16[1024]{0:T(1024)(128)(2,1)S(1)} %copy-done.5), channel_id=1, replica_groups=mesh['lat'=8,'tok'=4] {'lat'}, dimensions={0}, use_global_device_ids=true | all-gather | bytes 18432 | tf_op jit(solution)/shard_map/all_gather | solution.py:40
  95.9 9.9 %fusion = bf16[2048,512]{0,1:T(8,128)(2,1)} fusion(bf16[2048,2048]{1,0:T(8,128)(2,1)} %param.8, bf16[2048,512]{0,1:T(8,128)(2,1)S(1)} %bitcast.43, f32[2048]{0:T(1024)S(1)} %dynamic-slice_convert_fusion), kind=kOutput, calls=%fused_computation.8 | convolution fusion | flops 4299161600 | bytes 12591104 | tf_op jit(solution)/shard_map/dot_general | solution.py:47
  106.0 0.6 copy-done.4
  106.5 5.5 %all_gather.20 = s32[512,64]{0,1:T(8,128)S(1)} all-gather(s32[128,64]{0,1:T(8,128)S(1)} %copy-done.4), channel_id=1, replica_groups=mesh['lat'=8,'tok'=4] {'tok'}, dimensions={0}, use_global_device_ids=true | all-gather | bytes 163840 | tf_op jit(solution)/shard_map/all_gather | solution.py:39
  112.1 0.3 select_reduce_fusion
  112.4 0.1 shift_right_logical.11
  112.5 0.3 copy.16
  112.8 0.8 dynamic_slice.15
  113.6 21.5 %reduce-scatter.4.cloned.1.call-done = bf16[512,512]{0,1:T(8,128)(2,1)} async-done(((bf16[2048,512]{0,1:T(8,128)(2,1)}), bf16[512,512]{0,1:T(8,128)(2,1)}) %reduce-scatter.4.cloned.1.call-update) | async-done | bytes 524304 | tf_op jit(solution)/shard_map/reduce_scatter | solution.py:48
  135.1 2.1 multiply_convert_fusion.1
  137.2 22.7 %all-gather.7.cloned.1.call-done = bf16[2048,512]{0,1:T(8,128)(2,1)} async-done(((bf16[512,512]{0,1:T(8,128)(2,1)}), bf16[2048,512]{0,1:T(8,128)(2,1)}) %all-gather.7.cloned.1.call-update) | async-done | bytes 2097168 | tf_op jit(solution)/shard_map/all_gather | solution.py:50
  159.9 9.8 %fusion.1 = bf16[2048,512]{0,1:T(8,128)(2,1)} fusion(bf16[2048,512]{0,1:T(8,128)(2,1)} %all-gather.7.cloned.1.call-done, bf16[2048,2048]{1,0:T(8,128)(2,1)} %param.9), kind=kOutput, calls=%fused_computation.9 | convolution fusion | flops 4296015872 | bytes 12582912 | tf_op jit(solution)/shard_map/dot_general | solution.py:51
  169.9 68.3 %reduce-scatter.6.cloned.1.call-done = bf16[256,512]{0,1:T(8,128)(2,1)} async-done(((bf16[2048,512]{0,1:T(8,128)(2,1)}), bf16[256,512]{0,1:T(8,128)(2,1)}) %reduce-scatter.6.cloned.1.call-update) | async-done | bytes 262160 | tf_op jit(solution)/shard_map/reduce_scatter | solution.py:54
  238.2 1.7 subtract_convert_fusion.3
  240.1 51.0 %all-gather.9.cloned.1.call-done = bf16[2048,512]{0,1:T(8,128)(2,1)} async-done(((bf16[256,512]{0,1:T(8,128)(2,1)}), bf16[2048,512]{0,1:T(8,128)(2,1)}) %all-gather.9.cloned.1.call-update) | async-done | bytes 2097168 | tf_op jit(solution)/shard_map/all_gather | solution.py:60
  291.1 9.9 %fusion.2 = bf16[2048,512]{0,1:T(8,128)(2,1)} fusion(bf16[2048,512]{0,1:T(8,128)(2,1)} %all-gather.9.cloned.1.call-done, bf16[2048,2048]{1,0:T(8,128)(2,1)} %param.9), kind=kOutput, calls=%fused_computation.10 | convolution fusion | flops 4296015872 | bytes 12582912 | tf_op jit(solution)/shard_map/dot_general | solution.py:61
  301.0 0.2 all-gather.11.cloned.1.call-start
  301.2 29.5 %reduce-scatter.8.cloned.1.call-done = bf16[512,512]{0,1:T(8,128)(2,1)} async-done(((bf16[2048,512]{0,1:T(8,128)(2,1)}), bf16[512,512]{0,1:T(8,128)(2,1)}) %reduce-scatter.8.cloned.1.call-update) | async-done | bytes 524304 | tf_op jit(solution)/shard_map/reduce_scatter | solution.py:62
  330.7 2.0 multiply_convert_fusion
  332.8 2.1 convert_reduce_fusion
  334.9 0.1 copy-done.2
  335.0 8.4 %convolution_convert_fusion = bf16[2048,2048]{1,0:T(8,128)(2,1)} fusion(bf16[2048,512]{0,1:T(8,128)(2,1)} %all-gather.7.cloned.1.call-done, bf16[2048,512]{0,1:T(8,128)(2,1)S(1)} %copy-done.2), kind=kOutput, calls=%fused_computation | convolution fusion | flops 4299161600 | bytes 12582912 | tf_op jit(solution)/shard_map/dot_general | solution.py:65
  343.4 12.2 %all-gather.11.cloned.1.call-done = bf16[2048,512]{0,1:T(8,128)(2,1)} async-done(((bf16[512,512]{0,1:T(8,128)(2,1)}), bf16[2048,512]{0,1:T(8,128)(2,1)}) %all-gather.11.cloned.1.call-update) | async-done | bytes 2097168 | tf_op jit(solution)/shard_map/all_gather | solution.py:64
  355.5 2.0 convert_reduce_fusion.1
  357.5 4.6 %convolution_reduce_fusion = f32[2048]{0:T(1024)S(1)} fusion(bf16[2048,2048]{1,0:T(8,128)(2,1)} %param.8, bf16[1,2048]{1,0:T(2,128)(2,1)S(1)} %get-tuple-element.7, bf16[1,2048]{1,0:T(2,128)(2,1)S(1)} %get-tuple-element.6, bf16[1,2048]{1,0:T(2,128)(2,1)S(1)} %convert_element_type.154), kind=kOutput, calls=%fused_computation.13 | convolution fusion | flops 25206784 | bytes 8409088 | tf_op jit(solution)/shard_map/dot_general | solution.py:74
  362.1 21.6 %psum.7 = f32[2048]{0:T(1024)S(1)} all-reduce(f32[2048]{0:T(1024)S(1)} %convolution_reduce_fusion), channel_id=1, replica_groups=mesh['lat'=8,'tok'=4] {'lat'}, use_global_device_ids=true, to_apply=%region_7.8 | all-reduce | flops 2048 | bytes 16384 | tf_op jit(solution)/shard_map/psum | solution.py:75
  383.8 0.6 sub.66
  384.4 8.4 %convolution_convert_fusion.1 = bf16[2048,2048]{1,0:T(8,128)(2,1)} fusion(bf16[2048,512]{0,1:T(8,128)(2,1)} %all-gather.11.cloned.1.call-done, bf16[2048,512]{0,1:T(8,128)(2,1)S(1)} %bitcast.45, f32[2048]{0:T(1024)S(1)} %dynamic-slice_convert_fusion), kind=kOutput, calls=%fused_computation.1 | convolution fusion | flops 4302307328 | bytes 12591104 | tf_op jit(solution)/shard_map/dot_general | solution.py:77
  (30 shorter events, 0.7 us)
Async XLA Ops:
  7.2 55.0 %all-gather.5.cloned.1.call-start = ((), (), s32[]{:S(2)}) async-start(), calls=%async_computation.4 | async-start | bytes 2359296 | tf_op jit(solution)/shard_map/all_gather | solution.py:41
  66.1 3.8 copy-start.5
  66.1 29.8 %all-to-all-start = ((bf16[4,2048,128]{1,2,0:T(8,128)(2,1)}), bf16[4,2048,128]{1,2,0:T(8,128)(2,1)S(1)}, u32[]{:S(2)}, u32[]{:S(2)}) async-start(bf16[4,2048,128]{1,2,0:T(8,128)(2,1)} %copy.15), calls=%async_computation | async-start | bytes 4194304 | tf_op jit(solution)/shard_map/all_to_all | solution.py:42
  69.8 65.3 %reduce-scatter.4.cloned.1.call-start = ((), (), s32[]{:S(2)}) async-start(), calls=%async_computation.5 | async-start | bytes 2621440 | tf_op jit(solution)/shard_map/reduce_scatter | solution.py:48
  95.9 9.9 %copy-start = (bf16[4,2048,128]{1,2,0:T(8,128)(2,1)}, bf16[4,2048,128]{1,2,0:T(8,128)(2,1)S(1)}, u32[]{:S(2)}) copy-start(bf16[4,2048,128]{1,2,0:T(8,128)(2,1)S(1)} %all-to-all-done) | copy-start | bytes 6291460
  105.8 0.8 copy-start.4
  105.8 54.1 %all-gather.7.cloned.1.call-start = ((), (), s32[]{:S(2)}) async-start(), calls=%async_computation.6 | async-start | bytes 2621440 | tf_op jit(solution)/shard_map/all_gather | solution.py:50
  137.2 101.1 %reduce-scatter.6.cloned.1.call-start = ((), (), s32[]{:S(2)}) async-start(), calls=%async_computation.7 | async-start | bytes 2359296 | tf_op jit(solution)/shard_map/reduce_scatter | solution.py:54
  169.8 68.5 %copy-start.1 = (bf16[4,2048,128]{1,2,0:T(8,128)(2,1)S(1)}, bf16[4,2048,128]{1,2,0:T(8,128)(2,1)}, u32[]{:S(2)}) copy-start(bf16[4,2048,128]{1,2,0:T(8,128)(2,1)} %copy-done) | copy-start | bytes 6291460
  169.8 121.3 %all-gather.9.cloned.1.call-start = ((), (), s32[]{:S(2)}) async-start(), calls=%async_computation.8 | async-start | bytes 2359296 | tf_op jit(solution)/shard_map/all_gather | solution.py:60
  240.0 90.7 %reduce-scatter.8.cloned.1.call-start = ((), (), s32[]{:S(2)}) async-start(), calls=%async_computation.9 | async-start | bytes 2621440 | tf_op jit(solution)/shard_map/reduce_scatter | solution.py:62
  301.0 54.6 %all-gather.11.cloned.1.call-start = ((), (), s32[]{:S(2)}) async-start(), calls=%async_computation.10 | async-start | bytes 2621440 | tf_op jit(solution)/shard_map/all_gather | solution.py:64
  332.8 2.2 copy-start.2
  357.5 4.6 %copy-start.3 = (f32[2048]{0:T(1024)}, f32[2048]{0:T(1024)S(1)}, u32[]{:S(2)}) copy-start(f32[2048]{0:T(1024)S(1)} %convert_reduce_fusion.1) | copy-start | bytes 24580
Sparse Core Ops, SparseCore 0:
  10.1 51.9 all-gather.4
  105.9 29.1 reduce-scatter.3
  137.3 22.5 all-gather.6
  169.9 68.2 reduce-scatter.5
  240.9 50.1 all-gather.8
  301.1 29.5 reduce-scatter.7
  332.9 22.5 all-gather.10
where the time goes:
time: 400 us
  waiting for transfers between devices  260 us (65%)
  blocking collectives  53.1 us (13%)
  matrix products  50.9 us (13%)
  between operations  14.3 us (4%)
  other arithmetic  11 us (3%)
  local copies, waits for them, and re-layouts  5.95 us (1%)
  starting transfers between devices  4.21 us (1%)
    reduce_scatter x1, waiting for transfers between devices, on_device(): recon = lax.psum_scatter(recon_part, 'lat', scatter_dimension=0, tiled=True)  68.3 us
    all_gather x1, waiting for transfers between devices, on_device(): resid_full = lax.all_gather(resid, 'lat', axis=0, tiled=True)  54.2 us
    all_gather x1, waiting for transfers between devices, on_device(): errors = lax.all_gather(error_rows, 'lat', axis=0, tiled=True)  51 us
    reduce_scatter x1, waiting for transfers between devices, on_device(): gc = lax.psum_scatter(gc_part, 'tok', scatter_dimension=0, tiled=True)  29.5 us
    all_gather x1, blocking collectives, on_device(): bias_full = lax.all_gather(b_dec, 'lat', axis=0, tiled=True)  26 us
    all_gather x1, waiting for transfers between devices, on_device(): codes = lax.all_gather(codes_rows, 'tok', axis=0, tiled=True)  22.7 us
    psum x1, blocking collectives, on_device(): back = lax.psum(back, 'lat')  21.6 us
    reduce_scatter x1, waiting for transfers between devices, on_device(): pre = lax.psum_scatter(pre_part, 'tok', scatter_dimension=0, tiled=True)  21.5 us
  transfers between devices with their start and end apart: 8, of which 7 were waited for; matrix products, arithmetic and copies ran while one was open for 3% of the time, Pallas kernels for 0%

commit v1 on v0

--- a/solution.py
+++ b/solution.py
@@ -1,3 +1,4 @@
+import functools
 import jax
 import jax.numpy as jnp
 from jax import lax
@@ -5,6 +6,27 @@
 
 f32 = jnp.float32
 bf16 = jnp.bfloat16
+
+
+def wall_settle(original, link_axis):
+    big = lax.axis_size(link_axis)
+    tile_out, z1 = (big, lax.axis_index(link_axis))
+    prior, fresh = (original, 1)
+    while fresh < tile_out:
+        all_rows = []
+        t = 0
+        while t < tile_out:
+            all_rows.append((t, t ^ fresh))
+            t = t + 1
+        right_arr = lax.ppermute(prior, axis_name=link_axis, perm=all_rows)
+        parts_out = jnp.concatenate([prior, right_arr], axis=0)
+        v1 = jnp.concatenate([right_arr, prior], axis=0)
+        prior = jnp.where(z1 & fresh == 0, parts_out, v1)
+        fresh = 2 * fresh
+    return prior
+
+
+_make_digits = functools.partial(wall_settle, link_axis="lat")
 
 
 def active_rows(ids, base, rows):
@@ -38,7 +60,7 @@
     feats = width // lat_count
     ids_all = lax.all_gather(active_ids, "tok", axis=0, tiled=True).T
     bias_full = lax.all_gather(b_dec, "lat", axis=0, tiled=True)
-    resid_full = lax.all_gather(resid, "lat", axis=0, tiled=True)
+    resid_full = _make_digits(resid)
     resid_mine = lax.all_to_all(resid_full, "tok", split_axis=0, concat_axis=1, tiled=True)
     bias_mine = lax.dynamic_slice_in_dim(bias_full, tok_pos * width, width, 0)
     centred = (resid_mine.astype(f32) - bias_mine.astype(f32)[:, None]).astype(bf16)

time: 400 us -> 419 us (1.048)
  waiting for transfers between devices: 260 us -> 270 us
  starting transfers between devices: 4.21 us -> 11.6 us
    ppermute x0 -> x3, waiting for transfers between devices: none -> 62.2 us  [wall_settle(): right_arr = lax.ppermute(prior, axis_name=link_axis, perm=all_rows)]
    all_gather x1 -> x0, waiting for transfers between devices: 54.2 us -> none  [on_device(): resid_full = lax.all_gather(resid, 'lat', axis=0, tiled=True)]
    ppermute x0 -> x3, starting transfers between devices: none -> 7.45 us  [wall_settle(): right_arr = lax.ppermute(prior, axis_name=link_axis, perm=all_rows)]
  transfers between devices with their start and end apart: 8 -> 10, of which waited for: 7 -> 9; matrix products, arithmetic and copies ran while one was open for 3% -> 3% of each run, Pallas kernels for 0% -> 0%
where the time goes in v1:
time: 419 us
  waiting for transfers between devices  270 us (64%)
  blocking collectives  53.1 us (13%)
  matrix products  50.9 us (12%)
  other arithmetic  14.5 us (3%)
  between operations  14.3 us (3%)
  starting transfers between devices  11.6 us (3%)
  local copies, waits for them, and re-layouts  4.61 us (1%)
    reduce_scatter x1, waiting for transfers between devices, on_device(): recon = lax.psum_scatter(recon_part, 'lat', scatter_dimension=0, tiled=True)  68.3 us
    ppermute x3, waiting for transfers between devices, wall_settle(): right_arr = lax.ppermute(prior, axis_name=link_axis, perm=all_rows)  62.2 us
    all_gather x1, waiting for transfers between devices, on_device(): errors = lax.all_gather(error_rows, 'lat', axis=0, tiled=True)  50.9 us
    reduce_scatter x1, waiting for transfers between devices, on_device(): gc = lax.psum_scatter(gc_part, 'tok', scatter_dimension=0, tiled=True)  29.7 us
    all_gather x1, blocking collectives, on_device(): bias_full = lax.all_gather(b_dec, 'lat', axis=0, tiled=True)  26 us
    reduce_scatter x1, waiting for transfers between devices, on_device(): pre = lax.psum_scatter(pre_part, 'tok', scatter_dimension=0, tiled=True)  23.5 us
    all_gather x1, waiting for transfers between devices, on_device(): codes = lax.all_gather(codes_rows, 'tok', axis=0, tiled=True)  22.7 us
    psum x1, blocking collectives, on_device(): back = lax.psum(back, 'lat')  21.6 us
  transfers between devices with their start and end apart: 10, of which 9 were waited for; matrix products, arithmetic and copies ran while one was open for 3% of the time, Pallas kernels for 0%

profile of v1, /device:TPU:0, one launch (start us, length us, event | category | flops | bytes accessed | tf_op | source)
XLA Modules:
  0.0 418.5 jit_solution(8640735733563791027)
XLA Ops:
  7.2 3.0 collective-permute-start
  10.2 6.5 %collective-permute-done = bf16[1024,128]{1,0:T(8,128)(2,1)S(1)} collective-permute-done((bf16[1024,128]{1,0:T(8,128)(2,1)}, bf16[1024,128]{1,0:T(8,128)(2,1)S(1)}, u32[]{:S(2)}, u32[]{:S(2)}) %collective-permute-start) | collective-permute-done | bytes 262176 | tf_op jit(solution)/shard_map/ppermute | solution.py:21
  16.7 1.2 maximum_select_fusion.2
  17.9 1.9 collective-permute-start.1
  19.7 11.3 %collective-permute-done.1 = bf16[2048,128]{1,0:T(8,128)(2,1)S(1)} collective-permute-done((bf16[2048,128]{1,0:T(8,128)(2,1)S(1)}, bf16[2048,128]{1,0:T(8,128)(2,1)S(1)}, u32[]{:S(2)}, u32[]{:S(2)}) %collective-permute-start.1) | collective-permute-done | bytes 524320 | tf_op jit(solution)/shard_map/ppermute | solution.py:21
  31.3 2.6 collective-permute-start.2
  33.9 44.4 %collective-permute-done.2 = bf16[4096,128]{1,0:T(8,128)(2,1)} collective-permute-done((bf16[4096,128]{1,0:T(8,128)(2,1)S(1)}, bf16[4096,128]{1,0:T(8,128)(2,1)}, u32[]{:S(2)}, u32[]{:S(2)}) %collective-permute-start.2) | collective-permute-done | bytes 1048608 | tf_op jit(solution)/shard_map/ppermute | solution.py:21
  78.3 2.1 maximum_select_fusion
  80.4 2.6 copy.15
  83.0 3.7 all-to-all-start
  86.8 26.0 %all_gather.15 = bf16[8192]{0:T(1024)(128)(2,1)S(1)} all-gather(bf16[1024]{0:T(1024)(128)(2,1)S(1)} %copy-done.5), channel_id=1, replica_groups=mesh['lat'=8,'tok'=4] {'lat'}, dimensions={0}, use_global_device_ids=true | all-gather | bytes 18432 | tf_op jit(solution)/shard_map/all_gather | solution.py:62
  112.8 9.9 %fusion = bf16[2048,512]{0,1:T(8,128)(2,1)} fusion(bf16[2048,2048]{1,0:T(8,128)(2,1)} %param.8, bf16[2048,512]{0,1:T(8,128)(2,1)S(1)} %bitcast.44, f32[2048]{0:T(1024)S(1)} %dynamic-slice_convert_fusion), kind=kOutput, calls=%fused_computation.8 | convolution fusion | flops 4299161600 | bytes 12591104 | tf_op jit(solution)/shard_map/dot_general | solution.py:69
  123.5 5.4 %all_gather.16 = s32[512,64]{0,1:T(8,128)S(1)} all-gather(s32[128,64]{0,1:T(8,128)S(1)} %copy-done.4), channel_id=1, replica_groups=mesh['lat'=8,'tok'=4] {'tok'}, dimensions={0}, use_global_device_ids=true | all-gather | bytes 163840 | tf_op jit(solution)/shard_map/all_gather | solution.py:61
  129.7 0.8 dynamic_slice.15
  130.5 23.5 %reduce-scatter.4.cloned.1.call-done = bf16[512,512]{0,1:T(8,128)(2,1)} async-done(((bf16[2048,512]{0,1:T(8,128)(2,1)}), bf16[512,512]{0,1:T(8,128)(2,1)}) %reduce-scatter.4.cloned.1.call-update) | async-done | bytes 524304 | tf_op jit(solution)/shard_map/reduce_scatter | solution.py:70
  154.0 2.1 multiply_convert_fusion.1
  156.1 22.7 %all-gather.4.cloned.1.call-done = bf16[2048,512]{0,1:T(8,128)(2,1)} async-done(((bf16[512,512]{0,1:T(8,128)(2,1)}), bf16[2048,512]{0,1:T(8,128)(2,1)}) %all-gather.4.cloned.1.call-update) | async-done | bytes 2097168 | tf_op jit(solution)/shard_map/all_gather | solution.py:72
  178.8 9.8 %fusion.1 = bf16[2048,512]{0,1:T(8,128)(2,1)} fusion(bf16[2048,512]{0,1:T(8,128)(2,1)} %all-gather.4.cloned.1.call-done, bf16[2048,2048]{1,0:T(8,128)(2,1)} %param.9), kind=kOutput, calls=%fused_computation.9 | convolution fusion | flops 4296015872 | bytes 12582912 | tf_op jit(solution)/shard_map/dot_general | solution.py:73
  188.8 68.3 %reduce-scatter.6.cloned.1.call-done = bf16[256,512]{0,1:T(8,128)(2,1)} async-done(((bf16[2048,512]{0,1:T(8,128)(2,1)}), bf16[256,512]{0,1:T(8,128)(2,1)}) %reduce-scatter.6.cloned.1.call-update) | async-done | bytes 262160 | tf_op jit(solution)/shard_map/reduce_scatter | solution.py:76
  257.1 1.7 subtract_convert_fusion.3
  259.1 50.9 %all-gather.6.cloned.1.call-done = bf16[2048,512]{0,1:T(8,128)(2,1)} async-done(((bf16[256,512]{0,1:T(8,128)(2,1)}), bf16[2048,512]{0,1:T(8,128)(2,1)}) %all-gather.6.cloned.1.call-update) | async-done | bytes 2097168 | tf_op jit(solution)/shard_map/all_gather | solution.py:82
  310.0 9.9 %fusion.2 = bf16[2048,512]{0,1:T(8,128)(2,1)} fusion(bf16[2048,512]{0,1:T(8,128)(2,1)} %all-gather.6.cloned.1.call-done, bf16[2048,2048]{1,0:T(8,128)(2,1)} %param.9), kind=kOutput, calls=%fused_computation.10 | convolution fusion | flops 4296015872 | bytes 12582912 | tf_op jit(solution)/shard_map/dot_general | solution.py:83
  319.9 29.7 %reduce-scatter.8.cloned.1.call-done = bf16[512,512]{0,1:T(8,128)(2,1)} async-done(((bf16[2048,512]{0,1:T(8,128)(2,1)}), bf16[512,512]{0,1:T(8,128)(2,1)}) %reduce-scatter.8.cloned.1.call-update) | async-done | bytes 524304 | tf_op jit(solution)/shard_map/reduce_scatter | solution.py:84
  349.7 2.0 multiply_convert_fusion
  351.7 2.1 convert_reduce_fusion
  353.9 8.4 %convolution_convert_fusion = bf16[2048,2048]{1,0:T(8,128)(2,1)} fusion(bf16[2048,512]{0,1:T(8,128)(2,1)} %all-gather.4.cloned.1.call-done, bf16[2048,512]{0,1:T(8,128)(2,1)S(1)} %copy-done.2), kind=kOutput, calls=%fused_computation | convolution fusion | flops 4299161600 | bytes 12582912 | tf_op jit(solution)/shard_map/dot_general | solution.py:87
  362.3 12.2 %all-gather.8.cloned.1.call-done = bf16[2048,512]{0,1:T(8,128)(2,1)} async-done(((bf16[512,512]{0,1:T(8,128)(2,1)}), bf16[2048,512]{0,1:T(8,128)(2,1)}) %all-gather.8.cloned.1.call-update) | async-done | bytes 2097168 | tf_op jit(solution)/shard_map/all_gather | solution.py:86
  374.5 2.0 convert_reduce_fusion.1
  376.5 4.6 %convolution_reduce_fusion = f32[2048]{0:T(1024)S(1)} fusion(bf16[2048,2048]{1,0:T(8,128)(2,1)} %param.8, bf16[1,2048]{1,0:T(2,128)(2,1)S(1)} %get-tuple-element.7, bf16[1,2048]{1,0:T(2,128)(2,1)S(1)} %get-tuple-element.6, bf16[1,2048]{1,0:T(2,128)(2,1)S(1)} %convert_element_type.154), kind=kOutput, calls=%fused_computation.14 | convolution fusion | flops 25206784 | bytes 8409088 | tf_op jit(solution)/shard_map/dot_general | solution.py:96
  381.1 21.6 %psum.7 = f32[2048]{0:T(1024)S(1)} all-reduce(f32[2048]{0:T(1024)S(1)} %convolution_reduce_fusion), channel_id=1, replica_groups=mesh['lat'=8,'tok'=4] {'lat'}, use_global_device_ids=true, to_apply=%region_7.8 | all-reduce | flops 2048 | bytes 16384 | tf_op jit(solution)/shard_map/psum | solution.py:97
  402.7 0.6 sub.66
  403.3 8.4 %convolution_convert_fusion.1 = bf16[2048,2048]{1,0:T(8,128)(2,1)} fusion(bf16[2048,512]{0,1:T(8,128)(2,1)} %all-gather.8.cloned.1.call-done, bf16[2048,512]{0,1:T(8,128)(2,1)S(1)} %bitcast.46, f32[2048]{0:T(1024)S(1)} %dynamic-slice_convert_fusion), kind=kOutput, calls=%fused_computation.1 | convolution fusion | flops 4302307328 | bytes 12591104 | tf_op jit(solution)/shard_map/dot_general | solution.py:99
  (36 shorter events, 2.5 us)
Async XLA Ops:
  7.2 9.5 %collective-permute-start = (bf16[1024,128]{1,0:T(8,128)(2,1)}, bf16[1024,128]{1,0:T(8,128)(2,1)S(1)}, u32[]{:S(2)}, u32[]{:S(2)}) collective-permute-start(bf16[1024,128]{1,0:T(8,128)(2,1)} %param.6), channel_id=1, source_target_pairs={{0,4},{4,0},{8,12},{12,8},{16,20},{20,16},{24,28},{28,24},{1,5},{5... | collective-permute-start | bytes 786440 | tf_op jit(solution)/shard_map/ppermute | solution.py:21
  17.9 13.2 %collective-permute-start.1 = (bf16[2048,128]{1,0:T(8,128)(2,1)S(1)}, bf16[2048,128]{1,0:T(8,128)(2,1)S(1)}, u32[]{:S(2)}, u32[]{:S(2)}) collective-permute-start(bf16[2048,128]{1,0:T(8,128)(2,1)S(1)} %maximum_select_fusion.2), channel_id=1, source_target_pairs={{0,8},{4,12},{8,0},{12,4},{16,24},{20,28},{24,16},{28,20},{1,9},{5... | collective-permute-start | bytes 1572872 | tf_op jit(solution)/shard_map/ppermute | solution.py:21
  31.3 47.0 %collective-permute-start.2 = (bf16[4096,128]{1,0:T(8,128)(2,1)S(1)}, bf16[4096,128]{1,0:T(8,128)(2,1)}, u32[]{:S(2)}, u32[]{:S(2)}) collective-permute-start(bf16[4096,128]{1,0:T(8,128)(2,1)S(1)} %maximum_select_fusion.1), channel_id=1, source_target_pairs={{0,16},{4,20},{8,24},{12,28},{16,0},{20,4},{24,8},{28,12},{1,17},{... | collective-permute-start | bytes 3145736 | tf_op jit(solution)/shard_map/ppermute | solution.py:21
  83.0 3.8 copy-start.5
  83.0 29.8 %all-to-all-start = ((bf16[4,2048,128]{1,2,0:T(8,128)(2,1)}), bf16[4,2048,128]{1,2,0:T(8,128)(2,1)S(1)}, u32[]{:S(2)}, u32[]{:S(2)}) async-start(bf16[4,2048,128]{1,2,0:T(8,128)(2,1)} %copy.15), calls=%async_computation | async-start | bytes 4194304 | tf_op jit(solution)/shard_map/all_to_all | solution.py:64
  86.8 67.2 %reduce-scatter.4.cloned.1.call-start = ((), (), s32[]{:S(2)}) async-start(), calls=%async_computation.4 | async-start | bytes 2621440 | tf_op jit(solution)/shard_map/reduce_scatter | solution.py:70
  112.8 9.9 %copy-start = (bf16[4,2048,128]{1,2,0:T(8,128)(2,1)}, bf16[4,2048,128]{1,2,0:T(8,128)(2,1)S(1)}, u32[]{:S(2)}) copy-start(bf16[4,2048,128]{1,2,0:T(8,128)(2,1)S(1)} %all-to-all-done) | copy-start | bytes 6291460
  122.7 0.8 copy-start.4
  122.7 56.1 %all-gather.4.cloned.1.call-start = ((), (), s32[]{:S(2)}) async-start(), calls=%async_computation.5 | async-start | bytes 2621440 | tf_op jit(solution)/shard_map/all_gather | solution.py:72
  156.1 101.1 %reduce-scatter.6.cloned.1.call-start = ((), (), s32[]{:S(2)}) async-start(), calls=%async_computation.6 | async-start | bytes 2359296 | tf_op jit(solution)/shard_map/reduce_scatter | solution.py:76
  188.7 68.5 %copy-start.1 = (bf16[4,2048,128]{1,2,0:T(8,128)(2,1)S(1)}, bf16[4,2048,128]{1,2,0:T(8,128)(2,1)}, u32[]{:S(2)}) copy-start(bf16[4,2048,128]{1,2,0:T(8,128)(2,1)} %copy-done) | copy-start | bytes 6291460
  188.7 121.3 %all-gather.6.cloned.1.call-start = ((), (), s32[]{:S(2)}) async-start(), calls=%async_computation.7 | async-start | bytes 2359296 | tf_op jit(solution)/shard_map/all_gather | solution.py:82
  258.9 90.8 %reduce-scatter.8.cloned.1.call-start = ((), (), s32[]{:S(2)}) async-start(), calls=%async_computation.8 | async-start | bytes 2621440 | tf_op jit(solution)/shard_map/reduce_scatter | solution.py:84
  319.9 54.6 %all-gather.8.cloned.1.call-start = ((), (), s32[]{:S(2)}) async-start(), calls=%async_computation.9 | async-start | bytes 2621440 | tf_op jit(solution)/shard_map/all_gather | solution.py:86
  351.7 2.2 copy-start.2
  376.4 4.6 %copy-start.3 = (f32[2048]{0:T(1024)}, f32[2048]{0:T(1024)S(1)}, u32[]{:S(2)}) copy-start(f32[2048]{0:T(1024)S(1)} %convert_reduce_fusion.1) | copy-start | bytes 24580
Sparse Core Ops, SparseCore 0:
  122.8 31.1 reduce-scatter.3
  156.2 22.5 all-gather.3
  188.8 68.2 reduce-scatter.5
  259.8 50.1 all-gather.5
  320.0 29.6 reduce-scatter.7
  351.8 22.5 all-gather.7
